TPU v7x, 128 devices: a whole 4x4x4 slice. The times are simulated.
128 devices in a mesh: fsdp: 32 (over x, z, core), seq: 4 (over y).
Axes of the slice: x: 4, y: 4, z: 4, core: 2. Of those that a mesh axis runs over, the one named last changes fastest.
Arguments:
- inputs: bfloat16 [32, 4, 256, 1152], P('fsdp', 'seq'), may hold values from -4 to 4
- qkv_spatial: bfloat16 [32, 4, 256, 3456], P('fsdp', 'seq'), may hold values from -1.5 to 1.5
- tile_list: int32 [32, 4, 4, 3], P('fsdp', 'seq'), may hold values from 0 to 3, as said below
- tile_count: int32 [32, 4, 4], P('fsdp', 'seq'), may hold values from 1 to 3
- frame_count: int32 [32], P('fsdp'), may hold values from 2 to 4, as said below
- w_out: bfloat16 [1152, 1152], P('fsdp'), may hold values from -0.375 to 0.375
- w_qkv: bfloat16 [1152, 3456], P('fsdp'), may hold values from -0.1875 to 0.1875
- cot_y: bfloat16 [32, 4, 256, 1152], P('fsdp', 'seq'), may hold values from -6 to 6
- cot_out: bfloat16 [32, 4, 256, 1152], P('fsdp', None, 'seq'), may hold values from -6 to 6
Outputs:
- resid: bfloat16 [32, 4, 256, 1152], P('fsdp', 'seq')
- temporal_out: bfloat16 [32, 4, 256, 1152], P('fsdp', None, 'seq')
- grad_inputs: bfloat16 [32, 4, 256, 1152], P('fsdp', 'seq')
- grad_qkv: bfloat16 [32, 4, 256, 3456], P('fsdp', 'seq')
- grad_w_out: float32 [1152, 1152], P('fsdp')
- grad_w_qkv: float32 [1152, 3456], P('fsdp')
Inputs may be any that keep to these rules, and one draw needn't show every extreme that they name: `tile_list`: each list names 3 different tiles of the same frame. `frame_count`: frames from this count on are padding; some clip has no padding.
All inputs are finite; a program needn't handle non-finite values.
Results may differ from a plain program's by a relative error of at most 0.03.
Values may be sent and summed in bfloat16 or wider, within the bound.
No kernel may reach another device: no remote copies, remote signals or barrier semaphores. Data moves between devices by JAX's collectives and lax.ppermute only.
A program may use at most 192 MiB of HBM per device.

v0:
```python
import math

import jax
import jax.numpy as jnp
from jax import lax
from jax.sharding import PartitionSpec as P

D = 1152
HEADS = 16
HEAD_DIM = 72
TILE = 64
LIST_LEN = 3


EPS = 1e-06


def attend(queries, keys_in, values_in, valid, scale):
    scores = (
        jnp.einsum("...ld,...md->...lm", queries, keys_in, preferred_element_type=jnp.float32)
        * scale
    )
    raised = jnp.exp(scores) * valid
    probs = raised / jnp.sum(raised, axis=-1, keepdims=True)
    mixed = jnp.einsum(
        "...lm,...md->...ld",
        probs.astype(jnp.bfloat16),
        values_in,
        preferred_element_type=jnp.float32,
    )
    return (mixed.astype(jnp.bfloat16), probs)


def attend_back(grad_out, queries, keys_in, values_in, probs, scale):
    grad_probs = jnp.einsum(
        "...ld,...md->...lm", grad_out, values_in, preferred_element_type=jnp.float32
    )
    grad_values = jnp.einsum(
        "...lm,...ld->...md",
        probs.astype(jnp.bfloat16),
        grad_out,
        preferred_element_type=jnp.float32,
    )
    delta = jnp.sum(grad_probs * probs, axis=-1, keepdims=True)
    grad_scores = (probs * (grad_probs - delta) * scale).astype(jnp.bfloat16)
    grad_queries = jnp.einsum(
        "...lm,...md->...ld", grad_scores, keys_in, preferred_element_type=jnp.float32
    )
    grad_keys = jnp.einsum(
        "...lm,...ld->...md", grad_scores, queries, preferred_element_type=jnp.float32
    )
    return (grad_queries, grad_keys, grad_values)


def spatial_parts(frame_qkv, tile_list):
    tiles = frame_qkv.shape[0] // TILE
    parts = frame_qkv.reshape(tiles, TILE, 3, HEADS, HEAD_DIM).transpose(2, 3, 0, 1, 4)
    chosen_keys = parts[1][:, tile_list].reshape(HEADS, tiles, LIST_LEN * TILE, HEAD_DIM)
    chosen_values = parts[2][:, tile_list].reshape(HEADS, tiles, LIST_LEN * TILE, HEAD_DIM)
    return (parts[0], chosen_keys, chosen_values)


def spatial_forward(frame_qkv, tile_list, tile_count):
    tok_frame = frame_qkv.shape[0]
    queries, chosen_keys, chosen_values = spatial_parts(frame_qkv, tile_list)
    live = (jnp.arange(LIST_LEN)[None, :] < tile_count[:, None]).astype(jnp.float32)
    valid = jnp.repeat(live, TILE, axis=1)[None, :, None, :]
    mixed, probs = attend(queries, chosen_keys, chosen_values, valid, HEAD_DIM ** (-0.5))
    return (mixed.transpose(1, 2, 0, 3).reshape(tok_frame, D), probs)


def spatial_back(grad_attn, frame_qkv, tile_list, probs):
    tok_frame = frame_qkv.shape[0]
    tiles = tok_frame // TILE
    queries, chosen_keys, chosen_values = spatial_parts(frame_qkv, tile_list)
    grad_out = grad_attn.reshape(tiles, TILE, HEADS, HEAD_DIM).transpose(2, 0, 1, 3)
    grad_q, grad_k, grad_v = attend_back(
        grad_out, queries, chosen_keys, chosen_values, probs, HEAD_DIM ** (-0.5)
    )

    def spread(grad_chosen):
        pieces = grad_chosen.reshape(HEADS, tiles * LIST_LEN, TILE, HEAD_DIM).transpose(1, 0, 2, 3)
        summed = jax.ops.segment_sum(pieces, tile_list.reshape(-1), num_segments=tiles)
        return summed.transpose(1, 0, 2, 3)

    grads = jnp.stack([grad_q, spread(grad_k), spread(grad_v)])
    return grads.transpose(2, 3, 0, 1, 4).reshape(tok_frame, 3 * D).astype(jnp.bfloat16)


def temporal_parts(block_qkv):
    frames_n = block_qkv.shape[0]
    return block_qkv.reshape(frames_n, -1, 3, HEADS, HEAD_DIM).transpose(2, 1, 3, 0, 4)


def temporal_forward(block_qkv, count):
    frames_n = block_qkv.shape[0]
    parts = temporal_parts(block_qkv)
    valid = (jnp.arange(frames_n) < count).astype(jnp.float32)
    mixed, probs = attend(parts[0], parts[1], parts[2], valid, HEAD_DIM ** (-0.5))
    return (mixed.transpose(2, 0, 1, 3).reshape(frames_n, -1, D), probs)


def temporal_back(grad_out, block_qkv, probs):
    frames_n = block_qkv.shape[0]
    parts = temporal_parts(block_qkv)
    grad_heads = grad_out.reshape(frames_n, -1, HEADS, HEAD_DIM).transpose(1, 2, 0, 3)
    grads = jnp.stack(
        attend_back(grad_heads, parts[0], parts[1], parts[2], probs, HEAD_DIM ** (-0.5))
    )
    return grads.transpose(3, 1, 0, 2, 4).reshape(frames_n, -1, 3 * D).astype(jnp.bfloat16)


def normalize(rows):
    values = rows.astype(jnp.float32)
    centered = values - jnp.mean(values, axis=-1, keepdims=True)
    rstd_vals = lax.rsqrt(jnp.mean(centered * centered, axis=-1, keepdims=True) + EPS)
    return (centered * rstd_vals, rstd_vals)


def normalize_back(grad_hidden, normed, rstd_vals):
    inner = grad_hidden - jnp.mean(grad_hidden, axis=-1, keepdims=True)
    inner = inner - normed * jnp.mean(grad_hidden * normed, axis=-1, keepdims=True)
    return (rstd_vals * inner).astype(jnp.bfloat16)


def times_transposed(left, right):
    return lax.dot_general(
        left, right, (((1,), (1,)), ((), ())), preferred_element_type=jnp.float32
    )


def per_device(
    inputs, qkv_spatial, tile_list, tile_count, frame_count, w_out, w_qkv, cot_y, cot_out
):
    full_out, full_qkv = (
        lax.all_gather(w_out, "fsdp", axis=0, tiled=True),
        lax.all_gather(w_qkv, "fsdp", axis=0, tiled=True),
    )
    frames_dev = inputs.shape[1]
    tok_frame = inputs.shape[2]
    seq_count = lax.axis_size("seq")
    fsdp_count = lax.axis_size("fsdp")
    frames_all = frames_dev * seq_count
    tiles = tok_frame // TILE
    qkv_frames = qkv_spatial.reshape(frames_dev, tok_frame, 3 * D)
    lists = tile_list.reshape(frames_dev, tiles, LIST_LEN)
    counts = tile_count.reshape(frames_dev, tiles)
    attn, sprobs = jax.vmap(spatial_forward)(qkv_frames, lists, counts)
    attn_rows = attn.reshape(-1, D)
    resid = (
        inputs.reshape(-1, D).astype(jnp.float32)
        + jnp.dot(attn_rows, full_out, preferred_element_type=jnp.float32)
    ).astype(jnp.bfloat16)
    normed, rstd_vals = normalize(resid)
    hidden = normed.astype(jnp.bfloat16)
    proj_rows = jnp.dot(hidden, full_qkv, preferred_element_type=jnp.float32).astype(jnp.bfloat16)
    proj = lax.all_to_all(
        proj_rows.reshape(1, frames_dev, tok_frame, 3 * D),
        "seq",
        split_axis=2,
        concat_axis=1,
        tiled=True,
    )
    block = proj[0]
    tout, tprobs = temporal_forward(block, frame_count[0])
    grad_block = temporal_back(cot_out[0], block, tprobs)
    grad_back = lax.all_to_all(grad_block[None], "seq", split_axis=1, concat_axis=2, tiled=True)
    grad_proj = grad_back.reshape(-1, 3 * D)
    norm_back = normalize_back(times_transposed(grad_proj, full_qkv), normed, rstd_vals)
    grad_x = (cot_y.reshape(-1, D).astype(jnp.float32) + norm_back.astype(jnp.float32)).astype(
        jnp.bfloat16
    )
    grad_attn = times_transposed(grad_x, full_out).astype(jnp.bfloat16)
    grad_spatial = jax.vmap(spatial_back)(
        grad_attn.reshape(frames_dev, tok_frame, D), qkv_frames, lists, sprobs
    )
    term_out = lax.dot_general(
        attn_rows, grad_x, (((0,), (0,)), ((), ())), preferred_element_type=jnp.float32
    )
    term_qkv = lax.dot_general(
        hidden, grad_proj, (((0,), (0,)), ((), ())), preferred_element_type=jnp.float32
    )
    shares = lax.psum_scatter(
        jnp.concatenate([term_out, term_qkv], axis=1).astype(jnp.bfloat16),
        "fsdp",
        scatter_dimension=0,
        tiled=True,
    ).astype(jnp.float32)
    shares = lax.psum(shares.astype(jnp.bfloat16), "seq").astype(jnp.float32)
    factor = 1.0 / math.sqrt(fsdp_count * inputs.shape[0] * frames_all * tok_frame)
    return (
        resid.reshape(inputs.shape),
        tout[None],
        grad_x.reshape(inputs.shape),
        grad_spatial.reshape(qkv_spatial.shape),
        shares[:, :D] * factor,
        shares[:, D:] * factor,
    )


def solution(mesh):
    placed = (
        P("fsdp", "seq", None, None),
        P("fsdp", "seq", None, None),
        P("fsdp", "seq", None, None),
        P("fsdp", "seq", None),
        P("fsdp"),
        P("fsdp", None),
        P("fsdp", None),
        P("fsdp", "seq", None, None),
        P("fsdp", None, "seq", None),
    )
    return jax.shard_map(
        per_device,
        mesh=mesh,
        in_specs=placed,
        out_specs=(
            P("fsdp", "seq", None, None),
            P("fsdp", None, "seq", None),
            P("fsdp", "seq", None, None),
            P("fsdp", "seq", None, None),
            P("fsdp", None),
            P("fsdp", None),
        ),
        check_vma=False,
    )
```

profile of v0, /device:TPU:0, one launch (start us, length us, event | category | flops | bytes accessed | tf_op | source)
XLA Modules:
  0.0 533.4 jit_solution(15306088565514343253)
XLA Ops:
  8.7 6.9 %reshape_reshape.11 = bf16[1,4,64,3,16,72]{5,4,3,2,1,0:T(8,128)(2,1)S(1)} reshape(bf16[1,1,256,3456]{3,2,1,0:T(8,128)(2,1)} %param.10) | data formatting | bytes 3538944 | tf_op jit(solution)/shard_map/vmap()/reshape;reshape | solution.py:57
  20.1 2.7 gather_fusion.1
  22.8 4.6 copy.109
  27.6 2.7 gather_fusion
  30.3 2.6 copy.107
  32.9 4.4 bitcast_reduce_fusion
  41.3 16.7 %all-gather.5.cloned.1.call-done = bf16[32,36,1152]{2,1,0:T(8,128)(2,1)} async-done(((bf16[1,36,1152]{2,1,0:T(8,128)(2,1)}), bf16[32,36,1152]{2,1,0:T(8,128)(2,1)}) %all-gather.5.cloned.1.call-update) | async-done | bytes 2654224 | tf_op jit(solution)/shard_map/all_gather | solution.py:136
  58.0 5.2 reshape.292
  63.2 2.8 convert_reduce_fusion
  66.3 47.4 %all-gather.7.cloned.1.call-done = bf16[32,36,3456]{2,1,0:T(8,128)(2,1)} async-done(((bf16[1,36,3456]{2,1,0:T(8,128)(2,1)}), bf16[32,36,3456]{2,1,0:T(8,128)(2,1)}) %all-gather.7.cloned.1.call-update) | async-done | bytes 7962640 | tf_op jit(solution)/shard_map/all_gather | solution.py:137
  113.7 12.7 %reshape.294 = bf16[1152,3456]{1,0:T(8,128)(2,1)} reshape(bf16[32,36,3456]{2,1,0:T(8,128)(2,1)} %all-gather.7.cloned.1.call-done) | data formatting | bytes 15925248
  126.4 5.9 %fusion.2 = bf16[1,1,256,3456]{3,2,1,0:T(8,128)(2,1)S(1)} fusion(bf16[1152,3456]{1,0:T(8,128)(2,1)} %reshape.294, bf16[256,1152]{1,0:T(8,128)(2,1)S(1)} %get-tuple-element.15, f32[256]{0:T(256)S(1)} %add_rsqrt_fusion, f32[256]{0:T(256)S(1)} %broadcast_multiply_fusion.2), kind=kOutput, calls=%fused_computation.9 | convolution fusion | flops 2040496128 | bytes 10323968 | tf_op jit(solution)/shard_map/dot_general | solution.py:156
  132.3 2.7 copy.171
  135.6 11.9 %reduce.6 = bf16[256,3456]{1,0:T(8,128)(2,1)} reduce(bf16[256,1,1,3456]{3,2,1,0:T(2,128)(2,1)S(1)} %bitcast.191, bf16[]{:T(256)} %broadcast.198), dimensions={1,2}, to_apply=%bitcast.189.reduce_sub_computation | reduce | bytes 3538946
  147.5 3.9 reshape.297
  151.4 4.9 all-to-all-start
  156.4 2.8 reshape_squeeze.8
  159.8 20.1 %all-to-all-done = bf16[4,2,110592]{2,1,0:T(2,128)(2,1)} async-done(((bf16[4,2,110592]{2,1,0:T(2,128)(2,1)}), bf16[4,2,110592]{2,1,0:T(2,128)(2,1)}, u32[]{:S(2)}, u32[]{:S(2)}) %all-to-all-start) | async-done | bytes 1769504 | tf_op jit(solution)/shard_map/all_to_all | solution.py:157
  179.9 3.2 reshape.298
  183.1 11.7 %bitcast_reduce_fusion.1 = bf16[256,3456]{1,0:T(8,128)(2,1)} fusion(bf16[256,1,1,3456]{3,2,1,0:T(2,128)(2,1)S(1)} %reshape.298), kind=kLoop, calls=%fused_computation.113 | loop fusion | bytes 3538944 | tf_op jit(solution)/shard_map/all_to_all | solution.py:157
  194.9 6.9 %reshape_squeeze.7 = bf16[4,64,3,16,72]{4,3,2,1,0:T(8,128)(2,1)S(1)} reshape(bf16[256,3456]{1,0:T(8,128)(2,1)} %bitcast_reduce_fusion.1) | data formatting | bytes 3538944 | tf_op jit(solution)/shard_map/reshape;squeeze | solution.py:92
  201.8 4.0 copy.167
  208.4 2.6 fusion.44
  213.5 2.5 copy.114
  216.4 2.6 copy.120
  218.9 3.5 fusion.26
  226.8 2.8 fusion.27
  229.7 3.2 maximum_bitcast_fusion
  233.4 4.4 convert_element_type.132
  237.8 3.7 all-to-all-start.1
  243.6 2.9 fusion.24
  248.7 15.5 %all-to-all-done.1 = bf16[1,4,64,3456]{3,2,0,1:T(8,128)(2,1)S(1)} async-done(((bf16[1,4,64,3456]{3,2,0,1:T(8,128)(2,1)}), bf16[1,4,64,3456]{3,2,0,1:T(8,128)(2,1)S(1)}, u32[]{:S(2)}, u32[]{:S(2)}) %all-to-all-start.1) | async-done | bytes 1769504 | tf_op jit(solution)/shard_map/all_to_all | solution.py:167
  264.2 6.1 %fusion.72 = (f32[256]{0:T(256)S(1)}, f32[256]{0:T(256)S(1)}, f32[256,1152]{1,0:T(8,128)S(1)}) fusion(f32[256]{0:T(256)S(1)} %add_rsqrt_fusion, f32[256]{0:T(256)S(1)} %broadcast_multiply_fusion.2, bf16[256,1152]{1,0:T(8,128)(2,1)S(1)} %copy-done.5, bf16[256,3456]{1,0:T(8,128)(2,1)S(1)} %bitcast.201, bf16[1152,3456]{1,0:T(8,128)(2,1)} %reshape.294), kind=kOutput, calls=%fused_computation.112 | convolution fusion | flops 2040200704 | bytes 11505664 | tf_op jit(solution)/shard_map/dot_general | solution.py:127
  273.5 3.2 reshape_reshape.12
  276.7 7.4 %fusion.39 = f32[16,4,192,72]{3,2,1,0:T(8,128)} fusion(bf16[1,4,64,16,72]{4,3,2,1,0:T(8,128)(2,1)S(1)} %reshape_reshape.12, f32[16,4,192,64]{2,3,1,0:T(8,128)} %copy-done.8, f32[16,4,64]{2,1,0:T(4,128)S(1)} %copy-done.24, f32[4,192]{1,0:T(4,128)S(1)} %broadcast_in_dim.5), kind=kOutput, calls=%fused_computation.63 | convolution fusion | flops 116391936 | bytes 7293952 | tf_op jit(solution)/shard_map/vmap(...lm,...ld->...md)/dot_general | solution.py:38
  284.1 4.1 fusion.41
  288.2 5.6 %convolution_convert_fusion = bf16[1152,3456]{1,0:T(8,128)(2,1)} fusion(bf16[256,3456]{1,0:T(8,128)(2,1)S(1)} %bitcast.202, bf16[256,1152]{1,0:T(8,128)(2,1)S(1)} %copy-done.5, f32[256]{0:T(256)S(1)} %add_rsqrt_fusion, f32[256]{0:T(256)S(1)} %broadcast_multiply_fusion.2), kind=kOutput, calls=%fused_computation.5 | convolution fusion | flops 2043592704 | bytes 10323968 | tf_op jit(solution)/shard_map/dot_general | solution.py:180
  294.8 3.3 copy.135
  298.1 9.7 %pad_maximum_fusion = bf16[1152,4608]{1,0:T(8,128)(2,1)} fusion(bf16[1152,3456]{1,0:T(8,128)(2,1)} %convolution_convert_fusion, bf16[1152,1152]{1,0:T(8,128)(2,1)} %copy.135), kind=kLoop, calls=%fused_computation.6 | loop fusion | flops 21233664 | bytes 21233664 | tf_op jit(solution)/shard_map/concatenate | solution.py:184
  307.9 92.2 %fusion = bf16[40,4608]{1,0:T(8,128)(2,1)S(1)} fusion(bf16[1152,4608]{1,0:T(8,128)(2,1)} %pad_maximum_fusion), kind=kCustom, calls=%all-reduce-scatter | all-reduce-scatter fusion | flops 5898241 | bytes 10985984
  408.1 30.0 %fusion.8 = f32[16,4,192,72]{3,2,1,0:T(8,128)} fusion(f32[16,4,64,192]{3,2,1,0:T(8,128)} %fusion.41, bf16[1,3,16,4,64,72]{5,4,3,2,1,0:T(8,128)(2,1)} %bitcast.200, f32[16,4,192,64]{2,3,1,0:T(8,128)} %copy-done.8, f32[16,4,64]{2,1,0:T(4,128)S(1)} %copy-done.25, f32[4,192]{1,0:T(4,128)S(1)} %broadcast_in_dim.5), kind=kOutput, calls=%fused_computation.23 | convolution fusion | flops 121901248 | bytes 21438464 | tf_op jit(solution)/shard_map/vmap(...lm,...ld->...md)/dot_general | solution.py:49
  438.2 17.7 %concatenate.15 = bf16[164,4608]{1,0:T(8,128)(2,1)} concatenate(bf16[4,4608]{1,0:T(4,128)(2,1)} %collective-permute-done.3, bf16[40,4608]{1,0:T(8,128)(2,1)} %collective-permute-done.2, bf16[40,4608]{1,0:T(8,128)(2,1)} %collective-permute-done.1, bf16[40,4608]{1,0:T(8,128)(2,1)} %collective-permute-done, bf16[40,4608]{1,0:T(8,128)(2,1)S(1)} %fusion), dimensions={0} | concatenate | bytes 3022848
  457.8 26.9 %fusion.28 = bf16[1,1,16,4,64,72]{5,4,3,2,1,0:T(8,128)(2,1)} fusion(bf16[16,4,192,72]{3,2,1,0:T(8,128)(2,1)S(1)} %bitcast.195, f32[16,4,64,192]{3,2,1,0:T(8,128)} %fusion.41, f32[16,4,192,64]{2,3,1,0:T(8,128)} %copy-done.8, f32[16,4,64]{2,1,0:T(4,128)S(1)} %copy-done.26, f32[4,192]{1,0:T(4,128)S(1)} %broadcast_in_dim.5), kind=kOutput, calls=%fused_computation.47 | convolution fusion | flops 122196160 | bytes 8670208 | tf_op jit(solution)/shard_map/vmap(...lm,...md->...ld)/dot_general | solution.py:46
  484.8 6.6 %copy.132 = f32[12,16,64,72]{3,2,1,0:T(8,128)} copy(f32[12,16,64,72]{3,2,0,1:T(8,128)} %bitcast.204) | data formatting | bytes 7077888 | tf_op jit(solution)/shard_map/vmap()/transpose | solution.py:82
  491.7 8.4 %scatter_fusion.1 = f32[4,16,64,72]{3,2,1,0:T(8,128)S(1)} fusion(f32[4,16,64,72]{3,2,1,0:T(8,128)S(1)} %broadcast.139.clone, s32[12]{0:T(128)S(1)} %copy-done.29, f32[12,16,64,72]{3,2,1,0:T(8,128)} %copy.132), kind=kCustom, calls=%fused_computation.3 | custom fusion | flops 884736 | bytes 10616880 | tf_op jit(solution)/shard_map/vmap()/scatter-add | solution.py:83
  500.3 6.6 %copy.129 = f32[12,16,64,72]{3,2,1,0:T(8,128)} copy(f32[12,16,64,72]{3,2,0,1:T(8,128)} %bitcast.205) | data formatting | bytes 7077888 | tf_op jit(solution)/shard_map/vmap()/transpose | solution.py:82
  507.1 8.5 %scatter_fusion = f32[4,16,64,72]{3,2,1,0:T(8,128)S(1)} fusion(f32[4,16,64,72]{3,2,1,0:T(8,128)S(1)} %broadcast.139.clone.1, s32[12]{0:T(128)S(1)} %copy-done.29, f32[12,16,64,72]{3,2,1,0:T(8,128)} %copy.129), kind=kCustom, calls=%fused_computation.2 | custom fusion | flops 884736 | bytes 10616880 | tf_op jit(solution)/shard_map/vmap()/scatter-add | solution.py:83
  519.6 4.4 convert_element_type.139
  (129 shorter events, 46.0 us)
Async XLA Ops:
  7.2 50.8 %all-gather.5.cloned.1.call-start = ((), (), s32[]{:S(2)}) async-start(), calls=%async_computation.3 | async-start | bytes 3041280 | tf_op jit(solution)/shard_map/all_gather | solution.py:136
  7.9 105.8 %all-gather.7.cloned.1.call-start = ((), (), s32[]{:S(2)}) async-start(), calls=%async_computation.4 | async-start | bytes 9123840 | tf_op jit(solution)/shard_map/all_gather | solution.py:137
  15.6 2.5 copy-start.27
  22.8 4.6 copy-start.30
  32.9 4.4 copy-start
  32.9 4.4 copy-start.2
  37.3 2.0 copy-start.8
  37.3 2.0 copy-start.23
  41.3 24.7 %copy-start.6 = (bf16[256,1152]{1,0:T(8,128)(2,1)}, bf16[256,1152]{1,0:T(8,128)(2,1)S(1)}, u32[]{:S(2)}) copy-start(bf16[256,1152]{1,0:T(8,128)(2,1)S(1)} %reshape.237) | copy-start | bytes 1769476
  41.3 21.9 %copy-start.32 = (bf16[1,1,256,1152]{3,2,1,0:T(8,128)(2,1)S(1)}, bf16[1,1,256,1152]{3,2,1,0:T(8,128)(2,1)}, u32[]{:S(2)}) copy-start(bf16[1,1,256,1152]{3,2,1,0:T(8,128)(2,1)} %param.9) | copy-start | bytes 1769476
  66.0 60.4 %copy-start.4 = (bf16[256,1152]{1,0:T(8,128)(2,1)}, bf16[256,1152]{1,0:T(8,128)(2,1)S(1)}, u32[]{:S(2)}) copy-start(bf16[256,1152]{1,0:T(8,128)(2,1)S(1)} %get-tuple-element.15) | copy-start | bytes 1769476
  147.5 8.8 %copy-start.21 = (bf16[1,4,64,1152]{3,2,1,0:T(8,128)(2,1)S(1)}, bf16[1,4,64,1152]{3,2,1,0:T(8,128)(2,1)}, u32[]{:S(2)}) copy-start(bf16[1,4,64,1152]{3,2,1,0:T(8,128)(2,1)} %param.17) | copy-start | bytes 1769476
  151.4 28.5 %all-to-all-start = ((bf16[4,2,110592]{2,1,0:T(2,128)(2,1)}), bf16[4,2,110592]{2,1,0:T(2,128)(2,1)}, u32[]{:S(2)}, u32[]{:S(2)}) async-start(bf16[4,2,110592]{2,1,0:T(2,128)(2,1)} %reshape.297), calls=%async_computation | async-start | bytes 3538944 | tf_op jit(solution)/shard_map/all_to_all | solution.py:157
  205.9 2.6 copy-start.9
  205.9 2.6 copy-start.14
  211.0 7.9 %copy-start.10 = (bf16[4,64,3,16,72]{4,0,3,1,2:T(4,128)(2,1)S(1)}, bf16[4,64,3,16,72]{4,0,3,1,2:T(4,128)(2,1)}, u32[]{:S(2)}) copy-start(bf16[4,64,3,16,72]{4,0,3,1,2:T(4,128)(2,1)} %copy-done.9) | copy-start | bytes 5308420
  218.9 3.5 copy-start.17
  224.9 4.8 copy-start.19
  224.9 4.8 copy-start.20
  226.8 2.9 copy-start.15
  233.4 8.2 %copy-start.28 = (s32[1,1,4,3]{2,1,3,0:T(1,128)S(1)}, s32[1,1,4,3]{2,1,3,0:T(1,128)}, u32[]{:S(2)}) copy-start(s32[1,1,4,3]{2,1,3,0:T(1,128)} %param.11) | copy-start | bytes 148
  233.4 8.4 %copy-start.31 = (u32[128]{0:T(128)S(1)}, u32[128]{0:T(128)}, u32[]{:S(2)}) copy-start(u32[128]{0:T(128)} %constant.64) | copy-start | bytes 1540
  237.8 5.7 %copy-start.16 = (bf16[64,16,4,4]{2,3,1,0:T(4,128)(2,1)S(1)}, bf16[64,16,4,4]{2,3,1,0:T(4,128)(2,1)}, u32[]{:S(2)}) copy-start(bf16[64,16,4,4]{2,3,1,0:T(4,128)(2,1)} %copy-done.15) | copy-start | bytes 98308
  237.8 26.4 %all-to-all-start.1 = ((bf16[1,4,64,3456]{3,2,0,1:T(8,128)(2,1)}), bf16[1,4,64,3456]{3,2,0,1:T(8,128)(2,1)S(1)}, u32[]{:S(2)}, u32[]{:S(2)}) async-start(bf16[1,4,64,3456]{3,2,0,1:T(8,128)(2,1)} %bitcast.203), calls=%async_computation.1 | async-start | bytes 3538944 | tf_op jit(solution)/shard_map/all_to_all | solution.py:167
  241.5 282.5 %all-reduce.4.cloned.1.call-start = ((), (), s32[]{:S(2)}) async-start(), calls=%async_computation.2 | async-start | bytes 737280 | tf_op jit(solution)/shard_map/psum | solution.py:189
  243.6 20.7 %copy-start.5 = (bf16[256,1152]{1,0:T(8,128)(2,1)S(1)}, bf16[256,1152]{1,0:T(8,128)(2,1)}, u32[]{:S(2)}) copy-start(bf16[256,1152]{1,0:T(8,128)(2,1)} %copy-done.4) | copy-start | bytes 1769476
  264.2 6.1 %copy-start.22 = (bf16[1,1,256,1152]{3,2,1,0:T(8,128)(2,1)S(1)}, bf16[1,1,256,1152]{3,2,1,0:T(8,128)(2,1)}, u32[]{:S(2)}) copy-start(bf16[1,1,256,1152]{3,2,1,0:T(8,128)(2,1)} %param.16) | copy-start | bytes 1769476
  264.2 7.4 %copy-start.11 = (bf16[1152,1152]{1,0:T(8,128)(2,1)S(1)}, bf16[1152,1152]{1,0:T(8,128)(2,1)}, u32[]{:S(2)}) copy-start(bf16[1152,1152]{1,0:T(8,128)(2,1)} %reshape.292) | copy-start | bytes 7962628
  270.8 0.8 copy-start.12
  271.6 5.1 copy-start.24
  276.7 7.4 %copy-start.3 = (bf16[4,3,16,64,72]{4,3,1,0,2:T(8,128)(2,1)S(1)}, bf16[4,3,16,64,72]{4,3,1,0,2:T(8,128)(2,1)}, u32[]{:S(2)}) copy-start(bf16[4,3,16,64,72]{4,3,1,0,2:T(8,128)(2,1)} %copy.109) | copy-start | bytes 5308420
  288.2 5.7 %copy-start.7 = (bf16[256,1152]{1,0:T(8,128)(2,1)S(1)}, bf16[256,1152]{1,0:T(8,128)(2,1)}, u32[]{:S(2)}) copy-start(bf16[256,1152]{1,0:T(8,128)(2,1)} %copy-done.6) | copy-start | bytes 1769476
  288.2 5.7 %copy-start.13 = (bf16[256,1152]{1,0:T(8,128)(2,1)S(1)}, bf16[256,1152]{1,0:T(8,128)(2,1)}, u32[]{:S(2)}) copy-start(bf16[256,1152]{1,0:T(8,128)(2,1)} %copy-done.12) | copy-start | bytes 1769476
  307.9 100.3 %copy-start.25 = (f32[16,4,64]{2,1,0:T(4,128)S(1)}, f32[16,4,64]{2,1,0:T(4,128)}, u32[]{:S(2)}) copy-start(f32[16,4,64]{2,1,0:T(4,128)} %copy-done.23) | copy-start | bytes 49156
  400.1 38.1 %collective-permute-start.2 = (bf16[40,4608]{1,0:T(8,128)(2,1)S(1)}, bf16[40,4608]{1,0:T(8,128)(2,1)}, u32[]{:S(2)}, u32[]{:S(2)}) collective-permute-start(bf16[40,4608]{1,0:T(8,128)(2,1)S(1)} %fusion), channel_id=1, source_target_pairs={{0,12},{4,16},{8,20},{12,24},{16,28},{20,32},{24,36},{28,40},{32,4... | collective-permute-start | bytes 1105928
  402.2 36.0 %collective-permute-start.1 = (bf16[40,4608]{1,0:T(8,128)(2,1)S(1)}, bf16[40,4608]{1,0:T(8,128)(2,1)}, u32[]{:S(2)}, u32[]{:S(2)}) collective-permute-start(bf16[40,4608]{1,0:T(8,128)(2,1)S(1)} %fusion), channel_id=1, source_target_pairs={{0,8},{4,12},{8,16},{12,20},{16,24},{20,28},{24,32},{28,36},{32,40... | collective-permute-start | bytes 1105928
  404.2 34.0 %collective-permute-start = (bf16[40,4608]{1,0:T(8,128)(2,1)S(1)}, bf16[40,4608]{1,0:T(8,128)(2,1)}, u32[]{:S(2)}, u32[]{:S(2)}) collective-permute-start(bf16[40,4608]{1,0:T(8,128)(2,1)S(1)} %fusion), channel_id=1, source_target_pairs={{0,4},{4,8},{8,12},{12,16},{16,20},{20,24},{24,28},{28,32},{32,36}... | collective-permute-start | bytes 1105928
  406.2 31.9 %collective-permute-start.3 = (bf16[4,4608]{1,0:T(4,128)(2,1)S(1)}, bf16[4,4608]{1,0:T(4,128)(2,1)}, u32[]{:S(2)}, u32[]{:S(2)}) collective-permute-start(bf16[4,4608]{1,0:T(4,128)(2,1)S(1)} %slice.56), channel_id=1, source_target_pairs={{0,16},{4,20},{8,24},{12,28},{16,32},{20,36},{24,40},{28,44},{32,4... | collective-permute-start | bytes 110600
  438.2 19.7 %copy-start.1 = (bf16[4,3,16,64,72]{4,3,1,0,2:T(8,128)(2,1)S(1)}, bf16[4,3,16,64,72]{4,3,1,0,2:T(8,128)(2,1)}, u32[]{:S(2)}) copy-start(bf16[4,3,16,64,72]{4,3,1,0,2:T(8,128)(2,1)} %copy-done) | copy-start | bytes 5308420
  438.2 19.7 %copy-start.26 = (f32[16,4,64]{2,1,0:T(4,128)S(1)}, f32[16,4,64]{2,1,0:T(4,128)}, u32[]{:S(2)}) copy-start(f32[16,4,64]{2,1,0:T(4,128)} %copy-done.23) | copy-start | bytes 49156
  484.8 6.9 %copy-start.29 = (s32[12]{0:T(128)S(1)}, s32[12]{0:T(128)}, u32[]{:S(2)}) copy-start(s32[12]{0:T(128)} %fusion.64) | copy-start | bytes 148
  515.6 1.2 copy-start.18
Sparse Core Ops, SparseCore 0:
  10.3 47.6 all-gather.4
  60.2 53.4 all-gather.6
  457.9 40.4 all-reduce.3
where the time goes:
time: 544 us; the launch traced here: 533 us
  local copies, waits for them, and re-layouts  146 us (27%)
  matrix products  114 us (21%)
  waiting for transfers between devices  101 us (19%)
  blocking collectives  92.2 us (17%)
  other arithmetic  46.8 us (9%)
  starting transfers between devices  16.7 us (3%)
  between operations  15.8 us (3%)
    unnamed x1, blocking collectives  92.2 us
    unnamed x76, local copies, waits for them, and re-layouts  48.2 us
    all_gather x1, waiting for transfers between devices, per_device(): lax.all_gather(w_qkv, 'fsdp', axis=0, tiled=True)  47.4 us
    dot_general x2, matrix products, attend_back(): jnp.einsum('...lm,...ld->...md', grad_scores, queries, preferred_element_...  33.5 us
    dot_general x2, matrix products, attend_back(): jnp.einsum('...lm,...md->...ld', grad_scores, keys_in, preferred_element_...  29.3 us
    all_to_all x1, waiting for transfers between devices, per_device(): lax.all_to_all(proj_rows.reshape(1, frames_dev, tok_frame, 3 * D), 'seq',...  20.1 us
    scatter-add x3, other arithmetic, spread(): jax.ops.segment_sum(pieces, tile_list.reshape(-1), num_segments=tiles)  17.4 us
    all_gather x1, waiting for transfers between devices, per_device(): lax.all_gather(w_out, 'fsdp', axis=0, tiled=True)  16.7 us
  transfers between devices with their start and end apart: 9, of which 4 were waited for; matrix products, arithmetic and copies ran while one was open for 27% of the time, Pallas kernels for 0%

commit v1 on v0

v1 whole, which is shorter than its diff:
```python
import math

import jax
import jax.numpy as jnp
from jax import lax
from jax.experimental import pallas as pl
from jax.experimental.pallas import tpu as pltpu
from jax.sharding import PartitionSpec as P

D = 1152
HEADS = 16
HEAD_DIM = 72
TILE = 64
LIST_LEN = 3
HALF = D // 2
HALF_HEADS = HEADS // 2
EPS = 1e-06
SCALE = HEAD_DIM ** (-0.5)
F32 = jnp.float32
BF16 = jnp.bfloat16
VMEM = pl.BlockSpec(memory_space=pltpu.VMEM)
SMEM = pl.BlockSpec(memory_space=pltpu.SMEM)


def dot_nn(a, b):
    return lax.dot_general(a, b, (((1,), (0,)), ((), ())), preferred_element_type=F32)


def dot_nt(a, b):
    return lax.dot_general(a, b, (((1,), (1,)), ((), ())), preferred_element_type=F32)


def dot_tn(a, b):
    return lax.dot_general(a, b, (((0,), (0,)), ((), ())), preferred_element_type=F32)


def call(kernel, out_shape, operands, specs, scratch=(), limit=40, flops=0, nbytes=0):
    many = isinstance(out_shape, (list, tuple))
    return pl.pallas_call(
        kernel,
        out_shape=out_shape,
        in_specs=specs,
        out_specs=[VMEM] * len(out_shape) if many else VMEM,
        scratch_shapes=list(scratch),
        compiler_params=pltpu.CompilerParams(vmem_limit_bytes=limit << 20),
        cost_estimate=pl.CostEstimate(flops=flops, bytes_accessed=nbytes, transcendentals=0),
    )(*operands)


def head_window(head):
    low = head * HEAD_DIM
    start = low // 128 * 128
    stop = -(-(low + HEAD_DIM) // 128) * 128
    lane = lax.broadcasted_iota(jnp.int32, (1, stop - start), 1) + start
    inside = (lane >= low) & (lane < low + HEAD_DIM)
    return start, stop, inside


def key_mask(list_ref, count_ref, mask_ref):
    rows = mask_ref.shape[0]
    key_tile = lax.broadcasted_iota(jnp.int32, (TILE, rows), 1) // TILE
    for j in range(rows // TILE):
        live = jnp.zeros((TILE, rows), F32)
        for m in range(LIST_LEN):
            named = jnp.where(m < count_ref[j], list_ref[j, m], -1)
            live = jnp.where(key_tile == named, 1.0, live)
        mask_ref[j * TILE : (j + 1) * TILE, :] = live


def head_probs(qkv_ref, mask, start, stop, inside):
    queries = qkv_ref[:, start:stop]
    keys_in = jnp.where(inside, qkv_ref[:, D + start : D + stop], 0.0).astype(BF16)
    values_in = jnp.where(inside, qkv_ref[:, 2 * D + start : 2 * D + stop], 0.0).astype(BF16)
    raised = jnp.exp(dot_nt(queries, keys_in) * SCALE) * mask
    probs = raised * (1.0 / jnp.sum(raised, axis=-1, keepdims=True))
    return queries, keys_in, values_in, probs


def spatial_forward_kernel(list_ref, count_ref, qkv_ref, attn_ref, mask_ref):
    key_mask(list_ref, count_ref, mask_ref)
    attn_ref[...] = jnp.zeros_like(attn_ref)
    for head in range(HEADS):
        start, stop, inside = head_window(head)
        _, _, values_in, probs = head_probs(qkv_ref, mask_ref[...], start, stop, inside)
        mixed = dot_nn(probs.astype(BF16), values_in).astype(BF16)
        attn_ref[:, start:stop] = attn_ref[:, start:stop] + mixed


def spatial_back_kernel(list_ref, count_ref, qkv_ref, gx_ref, w_ref, out_ref, mask_ref, ga_ref):
    key_mask(list_ref, count_ref, mask_ref)
    ga_ref[...] = dot_nt(gx_ref[...], w_ref[...]).astype(BF16)
    out_ref[...] = jnp.zeros_like(out_ref)
    for head in range(HEADS):
        start, stop, inside = head_window(head)
        queries, keys_in, values_in, probs = head_probs(
            qkv_ref, mask_ref[...], start, stop, inside
        )
        grad = jnp.where(inside, ga_ref[:, start:stop], 0.0).astype(BF16)
        queries = jnp.where(inside, queries, 0.0).astype(BF16)
        grad_probs = dot_nt(grad, values_in)
        delta = jnp.sum(grad_probs * probs, axis=-1, keepdims=True)
        grad_scores = (probs * (grad_probs - delta) * SCALE).astype(BF16)
        for offset, part in (
            (0, dot_nn(grad_scores, keys_in)),
            (D, dot_tn(grad_scores, queries)),
            (2 * D, dot_tn(probs.astype(BF16), grad)),
        ):
            where = (slice(None), slice(offset + start, offset + stop))
            out_ref[where] = out_ref[where] + part.astype(BF16)


def resid_kernel(info_ref, x_ref, attn_ref, w_ref, resid_ref, *piece_refs):
    resid_ref[...] = (x_ref[...].astype(F32) + dot_nn(attn_ref[...], w_ref[...])).astype(BF16)
    n = len(piece_refs)
    for k, piece_ref in enumerate(piece_refs):
        at = lax.rem(info_ref[0] + k, n) * TILE
        piece_ref[...] = resid_ref[pl.ds(pl.multiple_of(at, TILE), TILE), :]


def normalize(rows):
    values = rows.astype(F32)
    centered = values - jnp.mean(values, axis=-1, keepdims=True)
    rstd_vals = lax.rsqrt(jnp.mean(centered * centered, axis=-1, keepdims=True) + EPS)
    return centered * rstd_vals, rstd_vals


def temporal_kernel(info_ref, count_ref, *refs):
    n = 4
    piece_refs = refs[: 2 * n]
    w_ref, cot_own_ref, cot_other_ref = refs[2 * n : 2 * n + 3]
    (tout_own_ref, tout_other_ref, hid_ref, gp_ref, gh_own_ref, gh_other_ref) = refs[
        2 * n + 3 : 2 * n + 9
    ]
    pj_ref, prod_ref, score_ref, weight_ref, wide_ref = refs[2 * n + 9 :]
    rows = TILE
    for i in range(2 * n):
        hid_ref[i * rows : (i + 1) * rows, :] = normalize(piece_refs[i][...])[0].astype(BF16)
    pj_ref[...] = dot_nn(hid_ref[...], w_ref[...]).astype(BF16)
    lane = lax.broadcasted_iota(jnp.int32, (HALF, 128), 0) // HEAD_DIM
    head = lax.broadcasted_iota(jnp.int32, (HALF, 128), 1)
    gather_heads = jnp.where(lane == head, 1.0, 0.0).astype(BF16)
    lane = lax.broadcasted_iota(jnp.int32, (128, HALF), 1) // HEAD_DIM
    head = lax.broadcasted_iota(jnp.int32, (128, HALF), 0)
    spread_heads = jnp.where(lane == head, 1.0, 0.0).astype(BF16)
    frames = [lax.rem(info_ref[0] + n - k, n) for k in range(n)]
    for clip in range(2):
        cot_ref = (cot_own_ref, cot_other_ref)[clip]
        tout_ref = (tout_own_ref, tout_other_ref)[clip]

        def part(k, which):
            at = (clip * n + k) * rows
            return pj_ref[at : at + rows, which * HALF : (which + 1) * HALF]

        queries = [part(k, 0) for k in range(n)]
        keys_in = [part(k, 1) for k in range(n)]
        values_in = [part(k, 2) for k in range(n)]
        cots = [cot_ref[frames[k]] for k in range(n)]
        for f in range(n):
            for g in range(n):
                at = (f * n + g) * rows
                prod_ref[at : at + rows, :] = queries[f] * keys_in[g]
                at += n * n * rows
                prod_ref[at : at + rows, :] = cots[f] * values_in[g]
        score_ref[...] = dot_nn(prod_ref[...], gather_heads)
        valid = [jnp.where(frames[k] < count_ref[clip], 1.0, 0.0) for k in range(n)]
        for f in range(n):
            raised, grad_probs = [], []
            for g in range(n):
                at = (f * n + g) * rows
                raised.append(jnp.exp(score_ref[at : at + rows, :] * SCALE) * valid[g])
                at += n * n * rows
                grad_probs.append(score_ref[at : at + rows, :])
            total = (raised[0] + raised[1]) + (raised[2] + raised[3])
            inverse = 1.0 / total
            probs = [r * inverse for r in raised]
            terms = [a * b for a, b in zip(grad_probs, probs)]
            delta = (terms[0] + terms[1]) + (terms[2] + terms[3])
            for g in range(n):
                at = (f * n + g) * rows
                weight_ref[at : at + rows, :] = probs[g].astype(BF16)
                at += n * n * rows
                weight_ref[at : at + rows, :] = (
                    probs[g] * (grad_probs[g] - delta) * SCALE
                ).astype(BF16)
        wide_ref[...] = dot_nn(weight_ref[...], spread_heads)

        def prob(f, g):
            at = (f * n + g) * rows
            return wide_ref[at : at + rows, :]

        def grad_score(f, g):
            at = (n * n + f * n + g) * rows
            return wide_ref[at : at + rows, :]

        for k in range(n):
            at = (clip * n + k) * rows
            out = sum(prob(k, g) * values_in[g].astype(F32) for g in range(n))
            tout_ref[frames[k]] = out.astype(BF16)
            grad_q = sum(grad_score(k, g) * keys_in[g].astype(F32) for g in range(n))
            grad_k = sum(grad_score(f, k) * queries[f].astype(F32) for f in range(n))
            grad_v = sum(prob(f, k) * cots[f].astype(F32) for f in range(n))
            gp_ref[at : at + rows, 0:HALF] = grad_q.astype(BF16)
            gp_ref[at : at + rows, HALF : 2 * HALF] = grad_k.astype(BF16)
            gp_ref[at : at + rows, 2 * HALF : 3 * HALF] = grad_v.astype(BF16)
    gh_other_ref[...] = dot_nt(gp_ref[n * rows :, :], w_ref[...]).astype(BF16)
    gh_own_ref[...] = dot_nt(gp_ref[: n * rows, :], w_ref[...])


def weight_term_kernel(left_ref, right_ref, out_ref):
    out_ref[...] = dot_tn(left_ref[...], right_ref[...]).astype(BF16)


def norm_back_kernel(*refs):
    n = 4
    piece_refs = refs[:n]
    own_ref, other_ref = refs[n : n + 2]
    for k in range(n):
        rows = slice(k * TILE, (k + 1) * TILE)
        grad_hidden = own_ref[rows, :] + other_ref[rows, :].astype(F32)
        normed, rstd_vals = normalize(piece_refs[k][...])
        inner = grad_hidden - jnp.mean(grad_hidden, axis=-1, keepdims=True)
        inner = inner - normed * jnp.mean(grad_hidden * normed, axis=-1, keepdims=True)
        refs[n + 2 + k][...] = (rstd_vals * inner).astype(BF16)


def grad_inputs_kernel(info_ref, cot_ref, *refs):
    n = 4
    out_ref, mine_ref, theirs_ref = refs[n:]
    for k in range(n):
        at = pl.multiple_of(lax.rem(info_ref[0] + k, n) * TILE, TILE)
        rows = pl.ds(at, TILE)
        out_ref[rows, :] = (cot_ref[rows, :].astype(F32) + refs[k][...].astype(F32)).astype(BF16)
    first, second = out_ref[:, :HALF], out_ref[:, HALF:]
    is_first = info_ref[1] == 0
    mine_ref[...] = jnp.where(is_first, first, second)
    theirs_ref[...] = jnp.where(is_first, second, first)


def per_device(
    inputs, qkv_spatial, tile_list, tile_count, frame_count, w_out, w_qkv, cot_y, cot_out
):
    seq_count = lax.axis_size("seq")
    fsdp_count = lax.axis_size("fsdp")
    tok_frame = inputs.shape[2]
    place = lax.axis_index("seq")
    core = lax.axis_index("fsdp") % 2
    info = jnp.stack([place, core]).astype(jnp.int32)
    pairs = [(i, i ^ 1) for i in range(fsdp_count)]
    groups = [list(range(c, fsdp_count, 2)) for c in range(2)]
    first_core = core == 0

    def swap(values):
        return lax.ppermute(values, "fsdp", pairs)

    def turn(values, k):
        return lax.ppermute(
            values, "seq", [(i, (i + k) % seq_count) for i in range(seq_count)]
        )

    def mine_theirs(first, second):
        return jnp.where(first_core, first, second), jnp.where(first_core, second, first)

    def shaped(shape, dtype=BF16):
        return jax.ShapeDtypeStruct(shape, dtype)

    def half_columns(c):
        cuts = [w_qkv[:, i * D + c * HALF : i * D + (c + 1) * HALF] for i in range(3)]
        return jnp.concatenate(cuts + [w_out[:, c * HALF : (c + 1) * HALF]], axis=1)

    mine, theirs = mine_theirs(half_columns(0), half_columns(1))
    got = swap(theirs)
    top, bottom = mine_theirs(mine, got)
    chip_rows = jnp.concatenate([top, bottom], axis=0)
    half_out = lax.all_gather(
        chip_rows[:, 3 * HALF :], "fsdp", axis=0, tiled=True, axis_index_groups=groups
    )
    half_qkv = lax.all_gather(
        chip_rows[:, : 3 * HALF], "fsdp", axis=0, tiled=True, axis_index_groups=groups
    )
    full_out = jnp.concatenate(mine_theirs(half_out, swap(half_out)), axis=1)

    cot_mine, cot_theirs = mine_theirs(cot_out[0][..., :HALF], cot_out[0][..., HALF:])
    cot_other = swap(cot_theirs)
    counts2 = jnp.concatenate([frame_count, swap(frame_count)])

    qkv = qkv_spatial.reshape(tok_frame, 3 * D)
    lists = tile_list.reshape(-1, LIST_LEN)
    counts = tile_count.reshape(-1)
    mask_scratch = pltpu.VMEM((tok_frame, tok_frame), F32)
    attn = call(
        spatial_forward_kernel,
        shaped((tok_frame, D)),
        (lists, counts, qkv),
        [SMEM, SMEM, VMEM],
        [mask_scratch],
        flops=4 * 10**9,
        nbytes=3 * 10**6,
    )
    attn_other = swap(attn)
    resid, *pieces = call(
        resid_kernel,
        [shaped((tok_frame, D))] + [shaped((TILE, D))] * seq_count,
        (info, inputs.reshape(tok_frame, D), attn, full_out),
        [SMEM, VMEM, VMEM, VMEM],
        flops=2 * 10**9,
        nbytes=4 * 10**6,
    )
    own = [pieces[0]] + [turn(pieces[k], k) for k in range(1, seq_count)]
    other = [swap(piece) for piece in own]
    wide = 2 * seq_count * seq_count * TILE
    rows = seq_count * TILE
    tout_own, tout_other, hidden, grad_proj, gh_own, gh_other = call(
        temporal_kernel,
        [
            shaped((seq_count, TILE, HALF)),
            shaped((seq_count, TILE, HALF)),
            shaped((2 * rows, D)),
            shaped((2 * rows, 3 * HALF)),
            shaped((rows, D), F32),
            shaped((rows, D)),
        ],
        (info, counts2, *own, *other, half_qkv, cot_mine, cot_other),
        [SMEM, SMEM] + [VMEM] * (2 * seq_count + 3),
        [
            pltpu.VMEM((2 * rows, 3 * HALF), BF16),
            pltpu.VMEM((wide, HALF), BF16),
            pltpu.VMEM((wide, 128), F32),
            pltpu.VMEM((wide, 128), BF16),
            pltpu.VMEM((wide, HALF), F32),
        ],
        flops=10**10,
        nbytes=10**7,
    )
    gh_got = swap(gh_other)
    tout_got = swap(tout_other)
    term_qkv = call(
        weight_term_kernel,
        shaped((D, 3 * HALF)),
        (hidden, grad_proj),
        [VMEM, VMEM],
        flops=2 * 10**9,
        nbytes=7 * 10**6,
    )
    backs = call(
        norm_back_kernel,
        [shaped((TILE, D))] * seq_count,
        (*own, gh_own, gh_got),
        [VMEM] * (seq_count + 2),
        flops=10**8,
        nbytes=3 * 10**6,
    )
    backs = [backs[0]] + [turn(backs[k], -k) for k in range(1, seq_count)]
    grad_x, gx_mine, gx_theirs = call(
        grad_inputs_kernel,
        [shaped((tok_frame, D)), shaped((tok_frame, HALF)), shaped((tok_frame, HALF))],
        (info, cot_y.reshape(tok_frame, D), *backs),
        [SMEM] + [VMEM] * (seq_count + 1),
        flops=10**7,
        nbytes=3 * 10**6,
    )
    gx_got = swap(gx_theirs)
    term_out = call(
        weight_term_kernel,
        shaped((D, HALF)),
        (jnp.concatenate([attn, attn_other], axis=0), jnp.concatenate([gx_mine, gx_got], axis=0)),
        [VMEM, VMEM],
        flops=10**9,
        nbytes=3 * 10**6,
    )
    grad_qkv = call(
        spatial_back_kernel,
        shaped((tok_frame, 3 * D)),
        (lists, counts, qkv, grad_x, full_out),
        [SMEM, SMEM] + [VMEM] * 3,
        [mask_scratch, pltpu.VMEM((tok_frame, D), BF16)],
        flops=10**10,
        nbytes=7 * 10**6,
    )

    def summed(term):
        share = lax.psum_scatter(
            term, "fsdp", scatter_dimension=0, tiled=True, axis_index_groups=groups
        )
        return lax.psum(share, "seq")

    share = jnp.concatenate([summed(term_qkv), summed(term_out)], axis=1)
    per = share.shape[0] // 2
    keep, send = mine_theirs(share[:per], share[per:])
    left, right = mine_theirs(keep, swap(send))
    factor = 1.0 / math.sqrt(fsdp_count * seq_count * tok_frame)
    left, right = left.astype(F32) * factor, right.astype(F32) * factor
    grad_w_qkv = jnp.concatenate(
        [side[:, i * HALF : (i + 1) * HALF] for i in range(3) for side in (left, right)], axis=1
    )
    grad_w_out = jnp.concatenate([left[:, 3 * HALF :], right[:, 3 * HALF :]], axis=1)
    tout = jnp.concatenate(mine_theirs(tout_own, tout_got), axis=-1)
    return (
        resid.reshape(inputs.shape),
        tout[None],
        grad_x.reshape(inputs.shape),
        grad_qkv.reshape(qkv_spatial.shape),
        grad_w_out,
        grad_w_qkv,
    )


def solution(mesh):
    placed = (
        P("fsdp", "seq", None, None),
        P("fsdp", "seq", None, None),
        P("fsdp", "seq", None, None),
        P("fsdp", "seq", None),
        P("fsdp"),
        P("fsdp", None),
        P("fsdp", None),
        P("fsdp", "seq", None, None),
        P("fsdp", None, "seq", None),
    )
    return jax.shard_map(
        per_device,
        mesh=mesh,
        in_specs=placed,
        out_specs=(
            P("fsdp", "seq", None, None),
            P("fsdp", None, "seq", None),
            P("fsdp", "seq", None, None),
            P("fsdp", "seq", None, None),
            P("fsdp", None),
            P("fsdp", None),
        ),
        check_vma=False,
    )
```

time: 544 us -> 374 us (0.69); the launches traced: 533 us -> 372 us
  waiting for transfers between devices: 101 us -> 271 us
  local copies, waits for them, and re-layouts: 146 us -> 30 us
  matrix products: 114 us -> 0 us
  blocking collectives: 92.2 us -> 0 us
  other arithmetic: 46.8 us -> 10.3 us
  Pallas kernels: 0 us -> 32.6 us
    unnamed x7, waiting for transfers between devices: 1.4 us -> 144 us
    dot_general x18 -> x0, matrix products: 114 us -> none  [the longest x2 33.5 us: attend_back(): jnp.einsum('...lm,...ld->...md', grad_scores, queries, preferred_element_...]
    unnamed x1 -> x0, blocking collectives: 92.2 us -> none
    psum x1, waiting for transfers between devices: 0.01 us -> 41.6 us  [summed(): return lax.psum(share, 'seq')]
    all_to_all x2 -> x0, waiting for transfers between devices: 35.6 us -> none  [the longest x1 20.1 us: per_device(): lax.all_to_all(proj_rows.reshape(1, frames_dev, tok_frame, 3 * D), 'seq',...]
    pallas_call x0 -> x8, Pallas kernels: none -> 32.6 us  [call(): pl.pallas_call(kernel, out_shape=out_shape, in_specs=specs, out_specs=[VM...]
    another operation x11 -> x0, local copies, waits for them, and re-layouts: 32.4 us -> none  [the longest x2 11 us: temporal_parts(): block_qkv.reshape(frames_n, -1, 3, HEADS, HEAD_DIM).transpose(2, 1, 3, 0, 4)]
    unnamed x76 -> x71, local copies, waits for them, and re-layouts: 48.2 us -> 22.2 us
  transfers between devices with their start and end apart: 9 -> 24, of which waited for: 4 -> 13; matrix products, arithmetic and copies ran while one was open for 27% -> 3% of each run, Pallas kernels for 0% -> 5%
where the time goes in v1:
time: 374 us; the launch traced here: 372 us
  waiting for transfers between devices  271 us (72%)
  Pallas kernels  32.6 us (9%)
  local copies, waits for them, and re-layouts  30 us (8%)
  between operations  14.7 us (4%)
  starting transfers between devices  13.1 us (4%)
  other arithmetic  10.3 us (3%)
    unnamed x7, waiting for transfers between devices  144 us
    all_gather x1, waiting for transfers between devices, per_device(): lax.all_gather(chip_rows[:, 3 * HALF:], 'fsdp', axis=0, tiled=True, axis_...  45.7 us
    psum x1, waiting for transfers between devices, summed(): return lax.psum(share, 'seq')  41.6 us
    pallas_call x8, Pallas kernels, call(): pl.pallas_call(kernel, out_shape=out_shape, in_specs=specs, out_specs=[VM...  32.6 us
    unnamed x71, local copies, waits for them, and re-layouts  22.2 us
    all_gather x1, waiting for transfers between devices, per_device(): lax.all_gather(chip_rows[:, :3 * HALF], 'fsdp', axis=0, tiled=True, axis_...  21.6 us
    ppermute x6, waiting for transfers between devices, turn(): lax.ppermute(values, 'seq', [(i, (i + k) % seq_count) for i in range(seq_...  12.3 us
    ppermute x6, starting transfers between devices, turn(): lax.ppermute(values, 'seq', [(i, (i + k) % seq_count) for i in range(seq_...  10.1 us
  transfers between devices with their start and end apart: 24, of which 13 were waited for; matrix products, arithmetic and copies ran while one was open for 3% of the time, Pallas kernels for 5%

profile of v1, /device:TPU:0, one launch (start us, length us, event | category | flops | bytes accessed | tf_op | source)
XLA Modules:
  0.0 371.6 jit_solution(9303463444159151539)
XLA Ops:
  7.2 1.1 fusion.3
  8.7 1.4 collective-permute-done
  11.9 45.7 %all-gather.3.cloned.1.call-done = bf16[1152,576]{1,0:T(8,128)(2,1)} async-done(((bf16[72,576]{1,0:T(8,128)(2,1)}), bf16[1152,576]{1,0:T(8,128)(2,1)}) %all-gather.3.cloned.1.call-update) | async-done | bytes 1327120 | tf_op jit(solution)/shard_map/all_gather | solution.py:274
  57.6 2.6 copy.17
  60.2 1.0 broadcast_select_fusion.4
  61.9 2.6 shard_map.136.attn_ref
  64.4 2.7 copy.18
  67.1 1.8 broadcast_select_fusion.1
  70.0 2.4 shard_map.137
  72.4 1.5 collective-permute-start.3
  73.9 2.7 collective-permute-start.4
  76.6 1.4 collective-permute-start.5
  78.1 1.2 collective-permute-done.2
  79.8 3.7 collective-permute-done.4.refs_2_
  89.4 21.6 %all-gather.5.cloned.1.call-done.refs_8_ = bf16[1152,1728]{1,0:T(8,128)(2,1)} async-done(((bf16[72,1728]{1,0:T(8,128)(2,1)}), bf16[1152,1728]{1,0:T(8,128)(2,1)}) %all-gather.5.cloned.1.call-update) | async-done | bytes 3981328 | tf_op jit(solution)/shard_map/all_gather | solution.py:277
  111.1 1.0 copy-done.5
  112.0 0.9 copy-done.7
  112.9 0.9 copy-done.9
  113.9 2.2 copy-done.10
  116.0 0.9 copy-done.18
  116.9 0.9 copy-done.20
  117.8 0.9 copy-done.22
  118.8 0.9 copy-done.24
  119.7 11.2 %shard_map.138 = (bf16[4,64,576]{2,1,0:T(8,128)(2,1)S(1)}, bf16[4,64,576]{2,1,0:T(8,128)(2,1)S(1)}, bf16[512,1152]{1,0:T(8,128)(2,1)S(1)}, bf16[512,1728]{1,0:T(...) custom-call(s32[2]{0:T(128)S(1)} %pad_add_fusion.info_ref, s32[2]{0:T(128)S(1)} %pad_add_fusion.1.count_ref, ...), custom_call_target="tpu_custom_call" | custom-call | flops 10000000000 | bytes 10000000 | tf_op jit(solution)/shard_map/pallas_call | solution.py:39
  130.8 1.0 copy-done.28
  132.5 1.5 collective-permute-done.12.refs_5_
  134.7 2.8 collective-permute-start.13
  139.2 4.9 %collective-permute-done.13.refs_1_ = bf16[64,1152]{1,0:T(8,128)(2,1)S(1)} collective-permute-done((bf16[64,1152]{1,0:T(8,128)(2,1)S(1)}, bf16[64,1152]{1,0:T(8,128)(2,1)S(1)}, u32[]{:S(2)}, u32[]{:S(2)}) %collective-permute-start.13) | collective-permute-done | bytes 147488 | tf_op jit(solution)/shard_map/ppermute | solution.py:256
  144.1 1.7 collective-permute-done.14.refs_2_
  145.8 2.0 collective-permute-done.15.refs_3_
  147.8 1.6 shard_map.140
  149.8 1.5 collective-permute-done.17
  151.4 1.1 shard_map.143
  152.6 1.1 copy-done.1
  153.7 1.5 copy-done.27
  155.2 1.3 copy-done.29
  156.5 2.4 shard_map.142
  158.9 2.0 copy-done
  160.9 0.9 copy-done.16
  162.0 62.7 %reduce-scatter.9.cloned.1.call-done = bf16[72,576]{1,0:T(8,128)(2,1)} async-done(((bf16[1152,576]{1,0:T(8,128)(2,1)}), bf16[72,576]{1,0:T(8,128)(2,1)}) %reduce-scatter.9.cloned.1.call-update) | async-done | bytes 82960
  224.7 81.2 %reduce-scatter.7.cloned.1.call-done = bf16[72,1728]{1,0:T(8,128)(2,1)} async-done(((bf16[1152,1728]{1,0:T(8,128)(2,1)}), bf16[72,1728]{1,0:T(8,128)(2,1)}) %reduce-scatter.7.cloned.1.call-update) | async-done | bytes 248848
  305.9 1.1 broadcast_select_fusion.3
  307.0 1.0 maximum_bitcast_fusion
  307.9 41.6 %all-reduce.5.cloned.1.call-done = (bf16[72,576]{1,0:T(8,128)(2,1)}, bf16[72,1728]{1,0:T(8,128)(2,1)}) async-done(((bf16[72,576]{1,0:T(8,128)(2,1)}, bf16[72,1728]{1,0:T(8,128)(2,1)}), (bf16[72,576]{1,0:T(8,128)(2,1)}, bf16[72,1728]{1,0:T(8,128)(2,1)})) %all-reduce.5.cloned.1.call-update) | async-done | bytes 331792 | tf_op jit(solution)/shard_map/psum | solution.py:384
  349.6 1.1 broadcast_select_fusion.6
  350.8 1.5 copy-done.12
  352.3 10.6 %shard_map.141 = bf16[256,3456]{1,0:T(8,128)(2,1)} custom-call(s32[4,3]{1,0:T(4,128)S(1)} %bitcast.16, s32[4]{0:T(128)S(1)} %bitcast.22, bf16[256,3456]{1,0:T(8,128)(2,1)S(1)} %bitcast.18, bf16[256,1152]{1,0:T(8,128)(2,1)S(1)} %copy-done.14, bf16[1152,1152]{1,0:T(8,128)(2,1)S(1)} %pad_maximum_fusion.w_ref), custom_call_target="tpu_custom_call" | custom-call | flops 10000000000 | bytes 7000000 | tf_op jit(solution)/shard_map/pallas_call | solution.py:39
  364.1 1.0 concatenate.43
  (108 shorter events, 14.7 us)
Async XLA Ops:
  7.2 50.4 %all-gather.3.cloned.1.call-start = ((), (), s32[]{:S(2)}) async-start(), calls=%async_computation.2 | async-start | bytes 1566720 | tf_op jit(solution)/shard_map/all_gather | solution.py:274
  8.7 1.5 collective-permute-start
  11.0 100.1 %all-gather.5.cloned.1.call-start = ((), (), s32[]{:S(2)}) async-start(), calls=%async_computation.3 | async-start | bytes 4386816 | tf_op jit(solution)/shard_map/all_gather | solution.py:277
  11.8 48.4 %copy-start.32 = (bf16[1,4,64,1152]{3,2,1,0:T(8,128)(2,1)S(1)}, bf16[1,4,64,1152]{3,2,1,0:T(8,128)(2,1)}, u32[]{:S(2)}) copy-start(bf16[1,4,64,1152]{3,2,1,0:T(8,128)(2,1)} %param.17) | copy-start | bytes 1769476
  11.8 49.9 %copy-start.34 = (s32[1,1,4,3]{2,1,3,0:T(1,128)S(1)}, s32[1,1,4,3]{2,1,3,0:T(1,128)}, u32[]{:S(2)}) copy-start(s32[1,1,4,3]{2,1,3,0:T(1,128)} %param.11) | copy-start | bytes 148
  11.8 50.1 %copy-start.11 = (bf16[1,1,256,3456]{3,2,1,0:T(8,128)(2,1)S(1)}, bf16[1,1,256,3456]{3,2,1,0:T(8,128)(2,1)}, u32[]{:S(2)}) copy-start(bf16[1,1,256,3456]{3,2,1,0:T(8,128)(2,1)} %param.10) | copy-start | bytes 5308420
  11.8 50.0 %copy-start.25 = (s32[1,1,4]{2,1,0:T(1,128)S(1)}, s32[1,1,4]{2,1,0:T(1,128)}, u32[]{:S(2)}) copy-start(s32[1,1,4]{2,1,0:T(1,128)} %param.12) | copy-start | bytes 52
  11.8 212.9 %reduce-scatter.9.cloned.1.call-start = ((), (), s32[]{:S(2)}) async-start(), calls=%async_computation.5 | async-start | bytes 1566720
  60.2 4.3 %collective-permute-start.1 = (bf16[1152,576]{0,1:T(8,128)(2,1)}, bf16[1152,576]{0,1:T(8,128)(2,1)}, u32[]{:S(2)}, u32[]{:S(2)}) collective-permute-start(bf16[1152,576]{0,1:T(8,128)(2,1)} %copy.17), channel_id=1, source_target_pairs={{0,4},{4,0},{8,12},{12,8},{16,20},{20,16},{24,28},{28,24},{32,36},... | collective-permute-start | bytes 3981320 | tf_op jit(solution)/shard_map/ppermute | solution.py:253
  61.2 25.6 %collective-permute-start.10 = (bf16[4,64,576]{2,1,0:T(8,128)(2,1)}, bf16[4,64,576]{2,1,0:T(8,128)(2,1)}, u32[]{:S(2)}, u32[]{:S(2)}) collective-permute-start(bf16[4,64,576]{2,1,0:T(8,128)(2,1)} %get-tuple-element.48), channel_id=1, source_target_pairs={{0,4},{4,0},{8,12},{12,8},{16,20},{20,16},{24,28},{28,24},{32,36},... | collective-permute-start | bytes 884744 | tf_op jit(solution)/shard_map/ppermute | solution.py:253
  64.4 2.7 copy-start.30
  68.9 1.1 copy-start.13
  72.4 7.1 %collective-permute-start.3 = (bf16[64,1152]{1,0:T(8,128)(2,1)S(1)}, bf16[64,1152]{1,0:T(8,128)(2,1)S(1)}, u32[]{:S(2)}, u32[]{:S(2)}) collective-permute-start(bf16[64,1152]{1,0:T(8,128)(2,1)S(1)} %get-tuple-element.26), channel_id=1, source_target_pairs={{0,1},{1,2},{2,3},{3,0},{4,5},{5,6},{6,7},{7,4},{8,9},{9,10},{10,1... | collective-permute-start | bytes 442376 | tf_op jit(solution)/shard_map/ppermute | solution.py:256
  73.9 9.6 %collective-permute-start.4 = (bf16[64,1152]{1,0:T(8,128)(2,1)S(1)}, bf16[64,1152]{1,0:T(8,128)(2,1)S(1)}, u32[]{:S(2)}, u32[]{:S(2)}) collective-permute-start(bf16[64,1152]{1,0:T(8,128)(2,1)S(1)} %get-tuple-element.27), channel_id=1, source_target_pairs={{0,2},{1,3},{2,0},{3,1},{4,6},{5,7},{6,4},{7,5},{8,10},{9,11},{10,... | collective-permute-start | bytes 442376 | tf_op jit(solution)/shard_map/ppermute | solution.py:256
  76.6 7.6 %collective-permute-start.5 = (bf16[64,1152]{1,0:T(8,128)(2,1)S(1)}, bf16[64,1152]{1,0:T(8,128)(2,1)S(1)}, u32[]{:S(2)}, u32[]{:S(2)}) collective-permute-start(bf16[64,1152]{1,0:T(8,128)(2,1)S(1)} %get-tuple-element.28), channel_id=1, source_target_pairs={{0,3},{1,0},{2,1},{3,2},{4,7},{5,4},{6,5},{7,6},{8,11},{9,8},{10,9... | collective-permute-start | bytes 442376 | tf_op jit(solution)/shard_map/ppermute | solution.py:256
  78.1 1.2 collective-permute-start.2
  79.3 7.5 %collective-permute-start.6 = (bf16[64,1152]{1,0:T(8,128)(2,1)S(1)}, bf16[64,1152]{1,0:T(8,128)(2,1)S(1)}, u32[]{:S(2)}, u32[]{:S(2)}) collective-permute-start(bf16[64,1152]{1,0:T(8,128)(2,1)S(1)} %get-tuple-element.25.refs_0_), channel_id=1, source_target_pairs={{0,4},{4,0},{8,12},{12,8},{16,20},{20,16},{24,28},{28,24},{32,36},... | collective-permute-start | bytes 442376 | tf_op jit(solution)/shard_map/ppermute | solution.py:253
  79.5 7.9 %collective-permute-start.7 = (bf16[64,1152]{1,0:T(8,128)(2,1)S(1)}, bf16[64,1152]{1,0:T(8,128)(2,1)S(1)}, u32[]{:S(2)}, u32[]{:S(2)}) collective-permute-start(bf16[64,1152]{1,0:T(8,128)(2,1)S(1)} %collective-permute-done.3.refs_1_), channel_id=1, source_target_pairs={{0,4},{4,0},{8,12},{12,8},{16,20},{20,16},{24,28},{28,24},{32,36},... | collective-permute-start | bytes 442376 | tf_op jit(solution)/shard_map/ppermute | solution.py:253
  83.5 4.6 %collective-permute-start.8 = (bf16[64,1152]{1,0:T(8,128)(2,1)S(1)}, bf16[64,1152]{1,0:T(8,128)(2,1)S(1)}, u32[]{:S(2)}, u32[]{:S(2)}) collective-permute-start(bf16[64,1152]{1,0:T(8,128)(2,1)S(1)} %collective-permute-done.4.refs_2_), channel_id=1, source_target_pairs={{0,4},{4,0},{8,12},{12,8},{16,20},{20,16},{24,28},{28,24},{32,36},... | collective-permute-start | bytes 442376 | tf_op jit(solution)/shard_map/ppermute | solution.py:253
  84.2 4.6 %collective-permute-start.9 = (bf16[64,1152]{1,0:T(8,128)(2,1)S(1)}, bf16[64,1152]{1,0:T(8,128)(2,1)S(1)}, u32[]{:S(2)}, u32[]{:S(2)}) collective-permute-start(bf16[64,1152]{1,0:T(8,128)(2,1)S(1)} %collective-permute-done.5.refs_3_), channel_id=1, source_target_pairs={{0,4},{4,0},{8,12},{12,8},{16,20},{20,16},{24,28},{28,24},{32,36},... | collective-permute-start | bytes 442376 | tf_op jit(solution)/shard_map/ppermute | solution.py:253
  111.1 1.0 copy-start.5
  112.0 0.9 copy-start.7
  113.9 2.2 copy-start.10
  130.8 1.0 copy-start.28
  131.9 17.6 %copy-start.3 = (bf16[4,64,576]{2,1,0:T(8,128)(2,1)}, bf16[4,64,576]{2,1,0:T(8,128)(2,1)S(1)}, u32[]{:S(2)}) copy-start(bf16[4,64,576]{2,1,0:T(8,128)(2,1)S(1)} %get-tuple-element.29) | copy-start | bytes 884740
  131.9 17.6 %copy-start.15 = (bf16[4,64,576]{2,1,0:T(8,128)(2,1)}, bf16[4,64,576]{2,1,0:T(8,128)(2,1)S(1)}, u32[]{:S(2)}) copy-start(bf16[4,64,576]{2,1,0:T(8,128)(2,1)S(1)} %get-tuple-element.30) | copy-start | bytes 884740
  131.9 17.6 %copy-start.26 = (bf16[512,1728]{1,0:T(8,128)(2,1)}, bf16[512,1728]{1,0:T(8,128)(2,1)S(1)}, u32[]{:S(2)}) copy-start(bf16[512,1728]{1,0:T(8,128)(2,1)S(1)} %get-tuple-element.39.right_ref) | copy-start | bytes 5308420
  131.9 15.9 %copy-start.2 = (bf16[1,1,256,1152]{3,2,1,0:T(8,128)(2,1)S(1)}, bf16[1,1,256,1152]{3,2,1,0:T(8,128)(2,1)}, u32[]{:S(2)}) copy-start(bf16[1,1,256,1152]{3,2,1,0:T(8,128)(2,1)} %param.16) | copy-start | bytes 1769476
  131.9 2.1 collective-permute-start.12
  132.0 17.8 %collective-permute-start.16 = (bf16[256,1152]{1,0:T(8,128)(2,1)S(1)}, bf16[256,1152]{1,0:T(8,128)(2,1)S(1)}, u32[]{:S(2)}, u32[]{:S(2)}) collective-permute-start(bf16[256,1152]{1,0:T(8,128)(2,1)S(1)} %shard_map.136.attn_ref), channel_id=1, source_target_pairs={{0,4},{4,0},{8,12},{12,8},{16,20},{20,16},{24,28},{28,24},{32,36},... | collective-permute-start | bytes 1769480 | tf_op jit(solution)/shard_map/ppermute | solution.py:253
  134.7 9.4 %collective-permute-start.13 = (bf16[64,1152]{1,0:T(8,128)(2,1)S(1)}, bf16[64,1152]{1,0:T(8,128)(2,1)S(1)}, u32[]{:S(2)}, u32[]{:S(2)}) collective-permute-start(bf16[64,1152]{1,0:T(8,128)(2,1)S(1)} %get-tuple-element.34), channel_id=1, source_target_pairs={{0,3},{1,0},{2,1},{3,2},{4,7},{5,4},{6,5},{7,6},{8,11},{9,8},{10,9... | collective-permute-start | bytes 442376 | tf_op jit(solution)/shard_map/ppermute | solution.py:256
  137.5 8.3 %collective-permute-start.14 = (bf16[64,1152]{1,0:T(8,128)(2,1)S(1)}, bf16[64,1152]{1,0:T(8,128)(2,1)S(1)}, u32[]{:S(2)}, u32[]{:S(2)}) collective-permute-start(bf16[64,1152]{1,0:T(8,128)(2,1)S(1)} %get-tuple-element.35), channel_id=1, source_target_pairs={{0,2},{1,3},{2,0},{3,1},{4,6},{5,7},{6,4},{7,5},{8,10},{9,11},{10,... | collective-permute-start | bytes 442376 | tf_op jit(solution)/shard_map/ppermute | solution.py:256
  138.3 9.5 %collective-permute-start.15 = (bf16[64,1152]{1,0:T(8,128)(2,1)S(1)}, bf16[64,1152]{1,0:T(8,128)(2,1)S(1)}, u32[]{:S(2)}, u32[]{:S(2)}) collective-permute-start(bf16[64,1152]{1,0:T(8,128)(2,1)S(1)} %get-tuple-element.36), channel_id=1, source_target_pairs={{0,1},{1,2},{2,3},{3,0},{4,5},{5,6},{6,7},{7,4},{8,9},{9,10},{10,1... | collective-permute-start | bytes 442376 | tf_op jit(solution)/shard_map/ppermute | solution.py:256
  149.4 1.9 collective-permute-start.17
  152.5 1.1 copy-start.1
  153.7 152.1 %reduce-scatter.7.cloned.1.call-start = ((), (), s32[]{:S(2)}) async-start(), calls=%async_computation.4 | async-start | bytes 4386816
  153.7 1.5 copy-start.27
  155.2 1.3 copy-start.29
  158.9 2.0 copy-start
  160.9 1.0 copy-start.16
  160.9 145.0 %copy-start.4 = (bf16[4,64,576]{2,1,0:T(8,128)(2,1)S(1)}, bf16[4,64,576]{2,1,0:T(8,128)(2,1)}, u32[]{:S(2)}) copy-start(bf16[4,64,576]{2,1,0:T(8,128)(2,1)} %copy-done.3) | copy-start | bytes 884740
  160.9 188.7 %all-reduce.5.cloned.1.call-start = ((), (), s32[]{:S(2)}) async-start(), calls=%async_computation.6 | async-start | bytes 700416 | tf_op jit(solution)/shard_map/psum | solution.py:384
  161.8 144.0 %collective-permute-start.11 = (bf16[4,64,576]{2,1,0:T(8,128)(2,1)S(1)}, bf16[4,64,576]{2,1,0:T(8,128)(2,1)}, u32[]{:S(2)}, u32[]{:S(2)}) collective-permute-start(bf16[4,64,576]{2,1,0:T(8,128)(2,1)S(1)} %copy-done.16), channel_id=1, source_target_pairs={{0,4},{4,0},{8,12},{12,8},{16,20},{20,16},{24,28},{28,24},{32,36},... | collective-permute-start | bytes 884744 | tf_op jit(solution)/shard_map/ppermute | solution.py:253
  306.9 43.9 %copy-start.14 = (bf16[256,1152]{1,0:T(8,128)(2,1)S(1)}, bf16[256,1152]{1,0:T(8,128)(2,1)}, u32[]{:S(2)}) copy-start(bf16[256,1152]{1,0:T(8,128)(2,1)} %get-tuple-element.37.gx_ref) | copy-start | bytes 1769476
  350.7 12.2 %collective-permute-start.18 = (bf16[36,2304]{1,0:T(8,128)(2,1)S(1)}, bf16[36,2304]{1,0:T(8,128)(2,1)S(1)}, u32[]{:S(2)}, u32[]{:S(2)}) collective-permute-start(bf16[36,2304]{1,0:T(8,128)(2,1)S(1)} %broadcast_select_fusion.6), channel_id=1, source_target_pairs={{0,4},{4,0},{8,12},{12,8},{16,20},{20,16},{24,28},{28,24},{32,36},... | collective-permute-start | bytes 497672 | tf_op jit(solution)/shard_map/ppermute | solution.py:253
  350.8 1.5 copy-start.12
  352.3 10.6 %copy-start.31 = (bf16[72,1728]{1,0:T(8,128)(2,1)S(1)}, bf16[72,1728]{1,0:T(8,128)(2,1)}, u32[]{:S(2)}) copy-start(bf16[72,1728]{1,0:T(8,128)(2,1)} %get-tuple-element.43) | copy-start | bytes 746500
  352.3 10.6 %copy-start.33 = (bf16[72,576]{1,0:T(8,128)(2,1)S(1)}, bf16[72,576]{1,0:T(8,128)(2,1)}, u32[]{:S(2)}) copy-start(bf16[72,576]{1,0:T(8,128)(2,1)} %get-tuple-element.42) | copy-start | bytes 248836
  (11 other events, 8.5 us)
Sparse Core Ops, SparseCore 0:
  11.1 46.4 all-gather.2
  60.4 50.6 all-gather.4
  153.8 70.8 reduce-scatter.8
  228.3 77.4 reduce-scatter.6
  308.2 41.3 all-reduce.4
